TPU v7x, 32 devices: a whole 2x2x4 slice. The times are simulated.
32 devices in a mesh: experts: 4 (over y, core), context: 8 (over z, x).
Axes of the slice: x: 2, y: 2, z: 4, core: 2. Of those that a mesh axis runs over, the one named last changes fastest.
Arguments:
- tokens: bfloat16 [2, 2048, 1024], P(None, ('experts', 'context')), may hold values from -6 to 6
- lengths: int32 [2], replicated, may hold values from 512 to 2048, as said below
- expert_index: int32 [2, 2048, 2], P(None, ('experts', 'context')), may hold values from 0 to 3, all different within a row
- cotangent: bfloat16 [2, 2048, 1024], P(None, ('experts', 'context')), may hold values from -18 to 18
- norm_attn: float32 [1024], replicated, may hold values from 0.5 to 1.5
- w_query: bfloat16 [1024, 1024], replicated, may hold values from -0.1875 to 0.1875
- w_key: bfloat16 [1024, 1024], replicated, may hold values from -0.1875 to 0.1875
- w_value: bfloat16 [1024, 1024], replicated, may hold values from -0.1875 to 0.1875
- w_out: bfloat16 [1024, 1024], replicated, may hold values from -0.75 to 0.75
- rel_bias: float32 [32, 16], replicated, may hold values from -3 to 3
- norm_ffn: float32 [1024], replicated, may hold values from 0.5 to 1.5
- router: float32 [1024, 4], replicated, may hold values from -0.13125 to 0.13125
- w_gate: bfloat16 [4, 1024, 2816], P('experts'), may hold values from -0.1875 to 0.1875
- w_up: bfloat16 [4, 1024, 2816], P('experts'), may hold values from -0.1875 to 0.1875
- w_down: bfloat16 [4, 2816, 1024], P('experts'), may hold values from -0.67578125 to 0.67578125
Outputs:
- mixed_out: bfloat16 [2, 2048, 1024], P(None, ('experts', 'context'))
- grad_tokens: float32 [2, 2048, 1024], P(None, ('experts', 'context'))
- grad_norm_attn: float32 [1024], replicated
- grad_w_query: float32 [1024, 1024], replicated
- grad_w_key: float32 [1024, 1024], replicated
- grad_w_value: float32 [1024, 1024], replicated
- grad_w_out: float32 [1024, 1024], replicated
- grad_rel_bias: float32 [32, 16], replicated
- grad_norm_ffn: float32 [1024], replicated
- grad_router: float32 [1024, 4], replicated
- grad_w_gate: float32 [4, 1024, 2816], P('experts', 'context')
- grad_w_up: float32 [4, 1024, 2816], P('experts', 'context')
- grad_w_down: float32 [4, 2816, 1024], P('experts', 'context')
Inputs may be any that keep to these rules, and one draw needn't show every extreme that they name: `lengths`: one sequence, drawn from the seed, is valid in all 2048 positions. `expert_index`: each token names two different experts.
All inputs are finite; a program needn't handle non-finite values.
Results may differ from a plain program's by a relative error of at most 0.03.
Values may be sent and summed in bfloat16 or wider, within the bound.
A program may use at most 384 MiB of HBM per device.

v0:
```python
import math

import jax
import jax.numpy as jnp
from jax import lax
from jax.sharding import PartitionSpec as P

MAXDIST = 128


norm_epsilon = 1e-06
mask_fill = -1e30
highest = lax.Precision.HIGHEST


def bucket_of(distance, bucket_count, reach):
    exact = bucket_count // 2
    if distance < exact:
        return distance
    level = exact + int(
        math.log(distance / exact) / math.log(reach / exact) * (bucket_count - exact)
    )
    return min(level, bucket_count - 1)


def bucket_edges(bucket_count, reach):
    edges = []
    for level in range(1, bucket_count):
        distance = 0
        while bucket_of(distance, bucket_count, reach) < level:
            distance += 1
        edges.append(distance)
    return edges


def relative_bucket(query_pos, key_pos, bucket_count):
    distance = jnp.maximum(query_pos[:, None] - key_pos[None, :], 0)
    bucket = jnp.zeros(distance.shape, jnp.int32)
    for edge in bucket_edges(bucket_count, MAXDIST):
        bucket = bucket + (distance >= edge).astype(jnp.int32)
    return bucket


def rms_norm(values, gain):
    inverse = lax.rsqrt(jnp.mean(values * values, axis=-1, keepdims=True) + norm_epsilon)
    return values * inverse * gain


def norm_back(values, gain, grad_in):
    inverse = lax.rsqrt(jnp.mean(values * values, axis=-1, keepdims=True) + norm_epsilon)
    normed = values * inverse
    grad_normed = grad_in * gain
    grad_values = inverse * (
        grad_normed - normed * jnp.mean(grad_normed * normed, axis=-1, keepdims=True)
    )
    return (grad_values, jnp.sum(grad_in * normed, 0))


def score_block(query_rows, key_rows, rel_bias, query_pos, key_pos, lengths, score_scale):
    raw_scores = (
        jnp.einsum("sqhd,skhd->sqhk", query_rows, key_rows, preferred_element_type=jnp.float32)
        * score_scale
    )
    bucket = relative_bucket(query_pos, key_pos, rel_bias.shape[0])
    onehot = (bucket[:, :, None] == jnp.arange(rel_bias.shape[0], dtype=jnp.int32)).astype(
        jnp.float32
    )
    bias_rows = jnp.einsum("qkb,bh->qhk", onehot, rel_bias, precision=highest)
    causal = (key_pos[None, :] <= query_pos[:, None])[None]
    inside = key_pos[None, None, :] < lengths[:, None, None]
    allowed = (causal & inside)[:, :, None, :]
    return (raw_scores + bias_rows[None], allowed, onehot)


def pair_grads(query_set, key_set, rel_bias, lengths, score_scale):
    query_rows, grad_rows, log_total, delta, query_pos = query_set
    key_rows, value_rows, key_pos = key_set
    scores, allowed, onehot = score_block(
        query_rows, key_rows, rel_bias, query_pos, key_pos, lengths, score_scale
    )
    weights = jnp.where(allowed, jnp.exp(scores - log_total[..., None]), 0.0)
    grad_value = jnp.einsum(
        "sqhk,sqhd->skhd",
        weights.astype(jnp.bfloat16),
        grad_rows,
        preferred_element_type=jnp.float32,
    )
    grad_weights = jnp.einsum(
        "sqhd,skhd->sqhk", grad_rows, value_rows, preferred_element_type=jnp.float32
    )
    grad_scores = (weights * (grad_weights - delta[..., None])).astype(jnp.bfloat16)
    grad_query = score_scale * jnp.einsum(
        "sqhk,skhd->sqhd", grad_scores, key_rows, preferred_element_type=jnp.float32
    )
    grad_key = score_scale * jnp.einsum(
        "sqhk,sqhd->skhd", grad_scores, query_rows, preferred_element_type=jnp.float32
    )
    grad_table = jnp.einsum(
        "sqhk,qkb->bh", grad_scores, onehot.astype(jnp.bfloat16), preferred_element_type=jnp.float32
    )
    return (grad_query, grad_key, grad_value, grad_table)


def dispatch_table(expert_index, live_rows, expert_count, capacity):
    picked = expert_index.reshape(-1)
    live_pairs = jnp.broadcast_to(live_rows[:, :, None], expert_index.shape).reshape(-1)
    chosen = (
        (picked[:, None] == jnp.arange(expert_count, dtype=jnp.int32)[None, :])
        & live_pairs[:, None]
    ).astype(jnp.int32)
    earlier = jnp.cumsum(chosen, axis=0) - chosen
    position_in = jnp.sum(earlier * chosen, -1)
    kept_pairs = live_pairs & (position_in < capacity)
    slot_of = jnp.where(kept_pairs, picked * capacity + position_in, -1)
    matches = slot_of[None, :] == jnp.arange(expert_count * capacity, dtype=jnp.int32)[:, None]
    table = jnp.any(matches.reshape(expert_count * capacity, -1, 2), -1).astype(jnp.float32)
    slot_ids = jnp.arange(expert_count * capacity, dtype=jnp.int32) // capacity
    slot_expert = (slot_ids[:, None] == jnp.arange(expert_count, dtype=jnp.int32)[None, :]).astype(
        jnp.float32
    )
    return (table, slot_expert)


def on_device(
    tokens,
    lengths,
    expert_index,
    cotangent,
    norm_attn,
    w_query,
    w_key,
    w_value,
    w_out,
    rel_bias,
    norm_ffn,
    router,
    w_gate,
    w_up,
    w_down,
):
    slot_count, per_slot, model_width = tokens.shape
    head_count = rel_bias.shape[1]
    head_size = model_width // head_count
    expert_count = router.shape[1]
    capacity = (10 * slot_count * per_slot + 4 * expert_count - 1) // (4 * expert_count)
    score_scale = head_size ** (-0.5)
    row_count = slot_count * per_slot
    shape_four = (slot_count, per_slot, head_count, head_size)
    shape_three = (slot_count, per_slot, model_width)
    device_at = lax.axis_index(("experts", "context"))
    positions = device_at * per_slot + jnp.arange(per_slot, dtype=jnp.int32)
    live_rows = positions[None, :] < lengths[:, None]
    keep_mask = live_rows.reshape(row_count, 1).astype(jnp.float32)
    inputs = tokens.reshape(row_count, model_width).astype(jnp.float32)
    normed = rms_norm(inputs, norm_attn).astype(jnp.bfloat16)
    query_flat = jnp.dot(normed, w_query, preferred_element_type=jnp.float32).astype(jnp.bfloat16)
    key_flat = jnp.dot(normed, w_key, preferred_element_type=jnp.float32).astype(jnp.bfloat16)
    value_flat = jnp.dot(normed, w_value, preferred_element_type=jnp.float32).astype(jnp.bfloat16)
    query_four = query_flat.reshape(shape_four)
    key_four = key_flat.reshape(shape_four)
    value_four = value_flat.reshape(shape_four)
    key_three = key_flat.reshape(shape_three)
    value_three = value_flat.reshape(shape_three)
    start_state = (
        jnp.zeros(shape_four, jnp.float32),
        jnp.full((slot_count, per_slot, head_count), mask_fill, jnp.float32),
        jnp.zeros((slot_count, per_slot, head_count), jnp.float32),
    )
    offset = jnp.int32(0)
    key_all = lax.all_gather(key_three, ("experts", "context"), axis=1, tiled=True)
    value_all = lax.all_gather(value_three, ("experts", "context"), axis=1, tiled=True)
    piece_rows = key_all.shape[1]
    block_rows = math.gcd(piece_rows, 8 * per_slot)

    def forward_visit(carried, block_id):
        running, running_max, denominator = carried
        local_at = block_id * block_rows
        key_rows = lax.dynamic_slice_in_dim(key_all, local_at, block_rows, 1).reshape(
            slot_count, block_rows, head_count, head_size
        )
        value_rows = lax.dynamic_slice_in_dim(value_all, local_at, block_rows, 1).reshape(
            slot_count, block_rows, head_count, head_size
        )
        key_pos = offset + local_at + jnp.arange(block_rows, dtype=jnp.int32)
        scores, allowed, _ = score_block(
            query_four, key_rows, rel_bias, positions, key_pos, lengths, score_scale
        )
        scores = jnp.where(allowed, scores, mask_fill)
        new_max = jnp.maximum(running_max, jnp.max(scores, -1))
        factor = jnp.exp(running_max - new_max)
        weights = jnp.where(allowed, jnp.exp(scores - new_max[..., None]), 0.0)
        denominator = denominator * factor + jnp.sum(weights, -1)
        running = running * factor[..., None] + jnp.einsum(
            "sqhk,skhd->sqhd",
            weights.astype(jnp.bfloat16),
            value_rows,
            preferred_element_type=jnp.float32,
        )
        return ((running, new_max, denominator), None)

    carried, _ = lax.scan(
        forward_visit, start_state, jnp.arange(piece_rows // block_rows, dtype=jnp.int32)
    )
    running, running_max, denominator = carried
    attended = running / denominator[..., None]
    log_total = running_max + jnp.log(denominator)
    attended_low = attended.reshape(row_count, model_width).astype(jnp.bfloat16)
    middle = inputs + jnp.dot(attended_low, w_out, preferred_element_type=jnp.float32)
    second_low = rms_norm(middle, norm_ffn).astype(jnp.bfloat16)
    second_wide = second_low.astype(jnp.float32)
    logits = jnp.dot(second_wide, router, precision=highest)
    gates = jax.nn.softmax(logits, axis=-1)
    table, slot_expert = dispatch_table(expert_index, live_rows, expert_count, capacity)
    table_low = table.astype(jnp.bfloat16)
    dispatched = jnp.dot(table_low, second_low, preferred_element_type=jnp.float32).astype(
        jnp.bfloat16
    )
    arrived = lax.all_to_all(
        dispatched.reshape(expert_count, capacity, model_width),
        "experts",
        split_axis=0,
        concat_axis=1,
        tiled=True,
    )[0]
    gate_pre = jnp.dot(arrived, w_gate[0], preferred_element_type=jnp.float32)
    up_pre = jnp.dot(arrived, w_up[0], preferred_element_type=jnp.float32)
    hidden_low = (jax.nn.gelu(gate_pre, approximate=True) * up_pre).astype(jnp.bfloat16)
    produced = jnp.dot(hidden_low, w_down[0], preferred_element_type=jnp.float32).astype(
        jnp.bfloat16
    )
    returned = lax.all_to_all(
        produced[None], "experts", split_axis=1, concat_axis=0, tiled=True
    ).reshape(expert_count * capacity, model_width)
    returned_wide = returned.astype(jnp.float32)
    slot_weight = jnp.sum(jnp.dot(table, gates, precision=highest) * slot_expert, -1)
    routed = jnp.dot(table.T, slot_weight[:, None] * returned_wide, precision=highest)
    result = ((middle + routed) * keep_mask).astype(jnp.bfloat16).reshape(shape_three)
    grad_result = cotangent.reshape(row_count, model_width).astype(jnp.float32) * keep_mask
    gathered_grad = jnp.dot(table, grad_result, precision=highest)
    grad_produced = (
        (slot_weight[:, None] * gathered_grad)
        .astype(jnp.bfloat16)
        .reshape(expert_count, capacity, model_width)
    )
    grad_arrived_out = lax.all_to_all(
        grad_produced, "experts", split_axis=0, concat_axis=1, tiled=True
    )[0]
    grad_slot_weight = jnp.sum(gathered_grad * returned_wide, -1)
    grad_hidden = jnp.dot(grad_arrived_out, w_down[0].T, preferred_element_type=jnp.float32)
    grad_w_down = jnp.dot(hidden_low.T, grad_arrived_out, preferred_element_type=jnp.float32)

    def activation(gate_in, up_in):
        return jax.nn.gelu(gate_in, approximate=True) * up_in

    _, activation_back = jax.vjp(activation, gate_pre, up_pre)
    grad_gate_pre, grad_up_pre = activation_back(grad_hidden)
    grad_gate_low = grad_gate_pre.astype(jnp.bfloat16)
    grad_up_low = grad_up_pre.astype(jnp.bfloat16)
    grad_w_gate = jnp.dot(arrived.T, grad_gate_low, preferred_element_type=jnp.float32)
    grad_w_up = jnp.dot(arrived.T, grad_up_low, preferred_element_type=jnp.float32)
    grad_arrived = (
        jnp.dot(grad_gate_low, w_gate[0].T, preferred_element_type=jnp.float32)
        + jnp.dot(grad_up_low, w_up[0].T, preferred_element_type=jnp.float32)
    ).astype(jnp.bfloat16)
    grad_returned = lax.all_to_all(
        grad_arrived[None], "experts", split_axis=1, concat_axis=0, tiled=True
    ).reshape(expert_count * capacity, model_width)
    expert_sums = (
        lax.psum_scatter(
            grad_w_gate[None].astype(jnp.bfloat16), "context", scatter_dimension=1, tiled=True
        ).astype(jnp.float32),
        lax.psum_scatter(
            grad_w_up[None].astype(jnp.bfloat16), "context", scatter_dimension=1, tiled=True
        ).astype(jnp.float32),
        lax.psum_scatter(
            grad_w_down[None].astype(jnp.bfloat16), "context", scatter_dimension=1, tiled=True
        ).astype(jnp.float32),
    )
    grad_second = jnp.dot(table_low.T, grad_returned, preferred_element_type=jnp.float32)
    grad_gates = jnp.dot(table.T, grad_slot_weight[:, None] * slot_expert, precision=highest)
    grad_logits = gates * (grad_gates - jnp.sum(gates * grad_gates, -1, keepdims=True))
    grad_router = jnp.dot(second_wide.T, grad_logits, precision=highest)
    grad_second = grad_second + jnp.dot(grad_logits, router.T, precision=highest)
    grad_middle_norm, grad_norm_ffn = norm_back(middle, norm_ffn, grad_second)
    grad_middle = grad_result + grad_middle_norm
    grad_middle_low = grad_middle.astype(jnp.bfloat16)
    grad_w_out = jnp.dot(attended_low.T, grad_middle_low, preferred_element_type=jnp.float32)
    grad_attended_low = jnp.dot(
        grad_middle_low, w_out.T, preferred_element_type=jnp.float32
    ).astype(jnp.bfloat16)
    grad_attended_four = grad_attended_low.reshape(shape_four)
    grad_attended_three = grad_attended_low.reshape(shape_three)
    delta = jnp.sum(grad_attended_four.astype(jnp.float32) * attended, -1)
    local_queries = (query_four, grad_attended_four, log_total, delta, positions)
    grad_start = (jnp.zeros(shape_four, jnp.float32), jnp.zeros(rel_bias.shape, jnp.float32))
    query_offset = jnp.int32(0)
    query_key_all = lax.all_gather(key_three, ("experts", "context"), axis=1, tiled=True)
    query_value_all = lax.all_gather(value_three, ("experts", "context"), axis=1, tiled=True)
    piece_rows = query_key_all.shape[1]
    query_block_rows = math.gcd(piece_rows, 8 * per_slot)

    def query_visit(carried, block_id):
        local_at = block_id * query_block_rows
        key_rows = lax.dynamic_slice_in_dim(query_key_all, local_at, query_block_rows, 1).reshape(
            slot_count, query_block_rows, head_count, head_size
        )
        value_rows = lax.dynamic_slice_in_dim(
            query_value_all, local_at, query_block_rows, 1
        ).reshape(slot_count, query_block_rows, head_count, head_size)
        key_pos = query_offset + local_at + jnp.arange(query_block_rows, dtype=jnp.int32)
        grad_query, _, _, grad_table = pair_grads(
            local_queries, (key_rows, value_rows, key_pos), rel_bias, lengths, score_scale
        )
        return ((carried[0] + grad_query, carried[1] + grad_table), None)

    carried, _ = lax.scan(
        query_visit, grad_start, jnp.arange(piece_rows // query_block_rows, dtype=jnp.int32)
    )
    grad_query_four, grad_table = carried
    log_whole, delta_whole = (
        lax.all_gather(log_total, ("experts", "context"), axis=1, tiled=True),
        lax.all_gather(delta, ("experts", "context"), axis=1, tiled=True),
    )
    local_keys = (key_four, value_four, positions)
    zero_four = jnp.zeros(shape_four, jnp.float32)
    key_offset = jnp.int32(0)
    query_all = lax.all_gather(
        query_flat.reshape(shape_three), ("experts", "context"), axis=1, tiled=True
    )
    grad_all = lax.all_gather(grad_attended_three, ("experts", "context"), axis=1, tiled=True)
    piece_rows = query_all.shape[1]
    key_block_rows = math.gcd(piece_rows, 8 * per_slot)

    def key_visit(carried, block_id):
        local_at = block_id * key_block_rows
        whole_at = key_offset + local_at
        query_rows = lax.dynamic_slice_in_dim(query_all, local_at, key_block_rows, 1).reshape(
            slot_count, key_block_rows, head_count, head_size
        )
        grad_rows = lax.dynamic_slice_in_dim(grad_all, local_at, key_block_rows, 1).reshape(
            slot_count, key_block_rows, head_count, head_size
        )
        log_rows = lax.dynamic_slice_in_dim(log_whole, whole_at, key_block_rows, 1)
        delta_rows = lax.dynamic_slice_in_dim(delta_whole, whole_at, key_block_rows, 1)
        query_pos = whole_at + jnp.arange(key_block_rows, dtype=jnp.int32)
        _, grad_key, grad_value, _ = pair_grads(
            (query_rows, grad_rows, log_rows, delta_rows, query_pos),
            local_keys,
            rel_bias,
            lengths,
            score_scale,
        )
        return ((carried[0] + grad_key, carried[1] + grad_value), None)

    carried, _ = lax.scan(
        key_visit, (zero_four, zero_four), jnp.arange(piece_rows // key_block_rows, dtype=jnp.int32)
    )
    grad_key_four, grad_value_four = carried
    grad_query_low = grad_query_four.reshape(row_count, model_width).astype(jnp.bfloat16)
    grad_key_low = grad_key_four.reshape(row_count, model_width).astype(jnp.bfloat16)
    grad_value_low = grad_value_four.reshape(row_count, model_width).astype(jnp.bfloat16)
    grad_w_query = jnp.dot(normed.T, grad_query_low, preferred_element_type=jnp.float32)
    grad_w_key = jnp.dot(normed.T, grad_key_low, preferred_element_type=jnp.float32)
    grad_w_value = jnp.dot(normed.T, grad_value_low, preferred_element_type=jnp.float32)
    grad_normed = (
        jnp.dot(grad_query_low, w_query.T, preferred_element_type=jnp.float32)
        + jnp.dot(grad_key_low, w_key.T, preferred_element_type=jnp.float32)
        + jnp.dot(grad_value_low, w_value.T, preferred_element_type=jnp.float32)
    )
    grad_input_norm, grad_norm_attn = norm_back(inputs, norm_attn, grad_normed)
    grad_tokens = (grad_middle + grad_input_norm).reshape(shape_three)
    dense = lax.psum(
        (
            grad_norm_attn,
            grad_w_query,
            grad_w_key,
            grad_w_value,
            grad_w_out,
            grad_table,
            grad_norm_ffn,
            grad_router,
        ),
        ("experts", "context"),
    )
    return (
        result,
        grad_tokens,
        dense[0],
        dense[1],
        dense[2],
        dense[3],
        dense[4],
        dense[5],
        dense[6],
        dense[7],
        expert_sums[0],
        expert_sums[1],
        expert_sums[2],
    )


def solution(mesh):
    placed = (
        P(None, ("experts", "context"), None),
        P(),
        P(None, ("experts", "context"), None),
        P(None, ("experts", "context"), None),
        P(),
        P(),
        P(),
        P(),
        P(),
        P(),
        P(),
        P(),
        P("experts", None, None),
        P("experts", None, None),
        P("experts", None, None),
    )
    return jax.shard_map(
        on_device,
        mesh=mesh,
        in_specs=placed,
        out_specs=(
            P(None, ("experts", "context"), None),
            P(None, ("experts", "context"), None),
            P(),
            P(),
            P(),
            P(),
            P(),
            P(),
            P(),
            P(),
            P("experts", "context", None),
            P("experts", "context", None),
            P("experts", "context", None),
        ),
        check_vma=False,
    )
```

profile of v0, /device:TPU:0, one launch (start us, length us, event | category | flops | bytes accessed | tf_op | source)
XLA Modules:
  0.0 1228.7 jit_solution(17484303035040869045)
XLA Ops:
  23.0 71.2 %all-gather.5.cloned.1.call-done = bf16[2,2048,1024]{2,0,1:T(2,128)(2,1)} async-done(((bf16[2,64,1024]{2,0,1:T(2,128)(2,1)}), bf16[2,2048,1024]{2,0,1:T(2,128)(2,1)}) %all-gather.5.cloned.1.call-update) | async-done | bytes 8388624 | tf_op jit(solution)/shard_map/all_gather | solution.py:170
  94.2 21.2 %copy.187 = bf16[2,2048,1024]{1,2,0:T(8,128)(2,1)} copy(bf16[2,2048,1024]{2,0,1:T(2,128)(2,1)} %all-gather.5.cloned.1.call-done) | data formatting | bytes 16777216
  115.3 58.4 %all-gather.7.cloned.1.call-done = bf16[2,2048,1024]{2,0,1:T(2,128)(2,1)} async-done(((bf16[2,64,1024]{2,0,1:T(2,128)(2,1)}), bf16[2,2048,1024]{2,0,1:T(2,128)(2,1)}) %all-gather.7.cloned.1.call-update) | async-done | bytes 8388624 | tf_op jit(solution)/shard_map/all_gather | solution.py:171
  173.8 21.3 %copy.189 = bf16[2,2048,1024]{1,2,0:T(8,128)(2,1)} copy(bf16[2,2048,1024]{2,0,1:T(2,128)(2,1)} %all-gather.7.cloned.1.call-done) | data formatting | bytes 16777216
  195.1 83.0 %while.41 = (s32[]{:T(128)}, f32[2,64,16,64]{1,3,2,0:T(8,128)}, f32[2,64,16]{1,2,0:T(8,128)S(1)}, f32[2,64,16]{1,2,0:T(8,128)S(1)}, s32[4]{0:T(128)S(1)}, /*inde...) while((s32[]{:T(128)}, f32[2,64,16,64]{1,3,2,0:T(8,128)}, ...), condition=%wide.region_4.5_spmd.clone, body=%wide.region_1.4_spmd.clone.sunk | while | flops 491171392 | bytes 73348160 | solution.py:201
  294.9 8.2 all-to-all-done.2
  322.7 9.2 fusion.192
  398.5 7.3 convert_bitcast_fusion.2
  405.9 7.4 convert_bitcast_fusion.1
  423.0 96.3 %all_gather.23 = f32[2,2048,16]{2,0,1:T(2,128)} all-gather(f32[2,64,16]{2,0,1:T(2,128)S(1)} %add.849), channel_id=1, replica_groups=mesh['experts'=4,'context'=8] {'experts','context'}, dimensions={1}, use_global_device_ids=true | all-gather | bytes 270336 | tf_op jit(solution)/shard_map/all_gather | solution.py:321
  523.0 7.3 convert_bitcast_fusion
  542.3 73.5 %while.42 = (s32[]{:T(128)}, f32[2,64,16,64]{1,3,2,0:T(8,128)}, f32[32,16]{0,1:T(8,128)}, s32[4]{0:T(128)S(1)}, bf16[2,2048,1024]{1,2,0:T(8,128)(2,1)}, /*index=...) while((s32[]{:T(128)}, f32[2,64,16,64]{1,3,2,0:T(8,128)}, ...), condition=%wide.region_19.20_spmd.clone, body=%wide.region_17.19_spmd.clone.sunk | while | flops 654215744 | bytes 52577412 | solution.py:316
  618.5 110.0 %all_gather.25 = f32[2,2048,16]{2,0,1:T(2,128)} all-gather(f32[2,64,16]{2,0,1:T(2,128)} %copy.212), channel_id=1, replica_groups=mesh['experts'=4,'context'=8] {'experts','context'}, dimensions={1}, use_global_device_ids=true | all-gather | bytes 270336 | tf_op jit(solution)/shard_map/all_gather | solution.py:322
  736.1 175.1 %while.43 = (s32[]{:T(128)}, f32[2,64,16,64]{1,3,2,0:T(8,128)}, f32[2,64,16,64]{1,3,2,0:T(8,128)S(1)}, s32[4]{0:T(128)S(1)}, bf16[2,2048,1024]{2,0,1:T(2,128)(2,...) while((s32[]{:T(128)}, f32[2,64,16,64]{1,3,2,0:T(8,128)}, ...), condition=%wide.region_21.22_spmd.clone, body=%wide.region_20.21_spmd.clone.sunk | while | flops 755663552 | bytes 51848704 | solution.py:355
  737.3 7.2 constant_dynamic-slice_fusion.14
  767.6 7.2 fusion.379
  781.0 7.2 constant_dynamic-slice_fusion.14
  811.3 7.3 fusion.379
  824.8 7.1 constant_dynamic-slice_fusion.14
  855.1 7.4 fusion.379
  868.6 7.1 constant_dynamic-slice_fusion.14
  898.8 7.3 fusion.379
  946.3 40.6 %all-reduce = (f32[1024]{0:T(1024)}, f32[32,16]{0,1:T(8,128)}, f32[1024]{0:T(1024)}, f32[1024,4]{0,1:T(4,128)}) all-reduce(f32[1024]{0:T(1024)S(1)} %get-tuple-element.568, f32[32,16]{0,1:T(8,128)S(1)} %copy-done.55, f32[1024]{0:T(1024)S(1)} %copy-done.47, ...), channel_id=1, replica_groups=mesh['experts'=4,'context'=8] {'experts','context'}, use_global_device_ids=true, to_apply=%region_24.25 | all-reduce | flops 6656 | bytes 53248 | tf_op jit(solution)/shard_map/psum | solution.py:372
  989.0 218.3 %all-reduce.4.cloned.1.call-done = (f32[1024,1024]{1,0:T(8,128)}, f32[1024,1024]{1,0:T(8,128)}, f32[1024,1024]{1,0:T(8,128)}, f32[1024,1024]{1,0:T(8,128)}) async-done(((f32[1024,1024]{1,0:T(8,128)}, f32[1024,1024]{1,0:T(8,128)}, f32[1024,1024]{1,0:T(8,128)}, f32[1024,1024]{1,0:T(8,128)}), (f32[1024,1024]{1,0:T(8,128)}, f32[1024,1024]{1,0:T(8,128)}, f32[1024,1024]{1,0:T(8,128)}, ...) | async-done | bytes 16777232 | tf_op jit(solution)/shard_map/psum | solution.py:372
  (522 shorter events, 469.8 us)
Async XLA Ops:
  7.2 87.0 %all-gather.5.cloned.1.call-start = ((), (), s32[]{:S(2)}) async-start(), calls=%async_computation.7 | async-start | bytes 8650752 | tf_op jit(solution)/shard_map/all_gather | solution.py:170
  13.9 159.8 %all-gather.7.cloned.1.call-start = ((), (), s32[]{:S(2)}) async-start(), calls=%async_computation.8 | async-start | bytes 8650752 | tf_op jit(solution)/shard_map/all_gather | solution.py:171
  16.2 719.9 %all-gather.9.cloned.1.call-start = ((), (), s32[]{:S(2)}) async-start(), calls=%async_computation.9 | async-start | bytes 8650752 | tf_op jit(solution)/shard_map/all_gather | solution.py:327
  22.7 372.9 %copy-start.65 = (f32[128]{0:T(128)}, f32[128]{0:T(128)S(1)}, u32[]{:S(2)}) copy-start(f32[128]{0:T(128)S(1)} %convert_element_type.849) | copy-start | bytes 1540
  22.9 369.6 %copy-start.37 = (pred[320,128]{1,0:T(8,128)(4,1)}, pred[320,128]{1,0:T(8,128)(4,1)S(1)}, u32[]{:S(2)}) copy-start(pred[320,128]{1,0:T(8,128)(4,1)S(1)} %fusion.222) | copy-start | bytes 122884
  115.3 79.7 %copy-start.31 = (f32[32,16]{0,1:T(8,128)S(1)}, f32[32,16]{0,1:T(8,128)}, u32[]{:S(2)}) copy-start(f32[32,16]{0,1:T(8,128)} %param.30) | copy-start | bytes 6148
  285.1 110.6 %copy-start.10 = (f32[128,1024]{1,0:T(8,128)}, f32[128,1024]{1,0:T(8,128)S(1)}, u32[]{:S(2)}) copy-start(f32[128,1024]{1,0:T(8,128)S(1)} %get-tuple-element.670) | copy-start | bytes 1572868
  286.3 108.0 %copy-start.45 = (f32[128,4]{0,1:T(4,128)}, f32[128,4]{0,1:T(4,128)S(1)}, u32[]{:S(2)}) copy-start(f32[128,4]{0,1:T(4,128)S(1)} %get-tuple-element.672) | copy-start | bytes 6148
  286.3 108.0 %copy-start.50 = (f32[128]{0:T(128)}, f32[128]{0:T(128)S(1)}, u32[]{:S(2)}) copy-start(f32[128]{0:T(128)S(1)} %get-tuple-element.671) | copy-start | bytes 1540
  286.3 107.9 %copy-start.58 = (f32[128]{0:T(128)}, f32[128]{0:T(128)S(1)}, u32[]{:S(2)}) copy-start(f32[128]{0:T(128)S(1)} %fusion.242) | copy-start | bytes 1540
  286.6 27.9 %copy-start.63 = (f32[320]{0:T(512)}, f32[320]{0:T(512)S(1)}, u32[]{:S(2)}) copy-start(f32[320]{0:T(512)S(1)} %fusion.213) | copy-start | bytes 3844
  288.7 14.5 %all-to-all-start.2 = ((bf16[4,80,1024]{2,1,0:T(8,128)(2,1)}), bf16[4,80,1024]{2,1,0:T(8,128)(2,1)}, u32[]{:S(2)}, u32[]{:S(2)}) async-start(bf16[4,80,1024]{2,1,0:T(8,128)(2,1)} %bitcast.372), calls=%async_computation.2 | async-start | bytes 1310720 | tf_op jit(solution)/shard_map/all_to_all | solution.py:245
  303.1 14.5 %all-to-all-start = ((bf16[4,80,1024]{2,1,0:T(8,128)(2,1)}), bf16[4,80,1024]{2,1,0:T(8,128)(2,1)}, u32[]{:S(2)}, u32[]{:S(2)}) async-start(bf16[4,80,1024]{2,1,0:T(8,128)(2,1)} %bitcast.371), calls=%async_computation | async-start | bytes 1310720 | tf_op jit(solution)/shard_map/all_to_all | solution.py:218
  317.7 14.3 %slice-start = ((s8[5767168]{0:T(1024)(128)(4,1)}), s8[4194304]{0:T(1024)(128)(4,1)S(1)}, s32[]{:S(2)}) async-start(s8[5767168]{0:T(1024)(128)(4,1)} %bitcast.380), calls=%async_computation.15 | async-start | bytes 8388608
  322.7 9.2 slice-start.1
  346.1 25.7 %all-to-all-start.1 = ((bf16[4,2,40960]{2,1,0:T(2,128)(2,1)}), bf16[4,2,40960]{2,1,0:T(2,128)(2,1)}, u32[]{:S(2)}, u32[]{:S(2)}) async-start(bf16[4,2,40960]{2,1,0:T(2,128)(2,1)} %reshape.895), calls=%async_computation.1 | async-start | bytes 1310720 | tf_op jit(solution)/shard_map/all_to_all | solution.py:231
  371.8 14.7 %all-to-all-start.3 = ((bf16[4,2,40960]{2,1,0:T(2,128)(2,1)}), bf16[4,2,40960]{2,1,0:T(2,128)(2,1)}, u32[]{:S(2)}, u32[]{:S(2)}) async-start(bf16[4,2,40960]{2,1,0:T(2,128)(2,1)} %reshape.897), calls=%async_computation.3 | async-start | bytes 1310720 | tf_op jit(solution)/shard_map/all_to_all | solution.py:265
  376.2 359.8 %all-gather.11.cloned.1.call-start = ((), (), s32[]{:S(2)}) async-start(), calls=%async_computation.10 | async-start | bytes 8650752 | tf_op jit(solution)/shard_map/all_gather | solution.py:330
  398.4 536.4 %reduce-scatter.4.cloned.1.call-start = ((), (), s32[]{:S(2)}) async-start(), calls=%async_computation.11 | async-start | bytes 6488064 | tf_op jit(solution)/shard_map/reduce_scatter | solution.py:269
  405.8 531.3 %reduce-scatter.6.cloned.1.call-start = ((), (), s32[]{:S(2)}) async-start(), calls=%async_computation.12 | async-start | bytes 6488064 | tf_op jit(solution)/shard_map/reduce_scatter | solution.py:272
  413.3 526.2 %reduce-scatter.8.cloned.1.call-start = ((), (), s32[]{:S(2)}) async-start(), calls=%async_computation.13 | async-start | bytes 6488064 | tf_op jit(solution)/shard_map/reduce_scatter | solution.py:275
  530.4 676.9 %all-reduce.4.cloned.1.call-start = ((), (), s32[]{:S(2)}) async-start(), calls=%async_computation.14 | async-start | bytes 33554432 | tf_op jit(solution)/shard_map/psum | solution.py:372
  533.7 8.6 copy-start.32
  941.9 45.0 %copy-start.13 = (f32[128,1024]{1,0:T(8,128)S(1)}, f32[128,1024]{1,0:T(8,128)}, u32[]{:S(2)}) copy-start(f32[128,1024]{1,0:T(8,128)} %copy-done.12) | copy-start | bytes 1572868
  (84 other events, 311.1 us)
Sparse Core Ops, SparseCore 0:
  14.0 80.1 all-gather.4
  97.7 75.9 all-gather.6
  176.8 76.0 all-gather.8
  398.5 96.6 all-gather.10
  498.7 113.5 reduce-scatter.3
  615.9 132.6 reduce-scatter.5
  752.1 110.0 reduce-scatter.7
  927.2 280.0 all-reduce.3
where the time goes:
time: 1240 us; the launch traced here: 1230 us
  waiting for transfers between devices  366 us (30%)
  local copies, waits for them, and re-layouts  261 us (21%)
  matrix products  252 us (20%)
  blocking collectives  247 us (20%)
  other arithmetic  61 us (5%)
  starting transfers between devices  17.6 us (1%)
  between operations  15.3 us (1%)
    psum x1, waiting for transfers between devices, on_device(): lax.psum((grad_norm_attn, grad_w_query, grad_w_key, grad_w_value, grad_w_...  218 us
    all_gather x1, blocking collectives, on_device(): lax.all_gather(delta, ('experts', 'context'), axis=1, tiled=True)  110 us
    all_gather x1, blocking collectives, on_device(): lax.all_gather(log_total, ('experts', 'context'), axis=1, tiled=True)  96.3 us
    unnamed x147, local copies, waits for them, and re-layouts  90.3 us
    all_gather x1, waiting for transfers between devices, on_device(): lax.all_gather(key_three, ('experts', 'context'), axis=1, tiled=True)  71.2 us
    all_gather x1, waiting for transfers between devices, on_device(): lax.all_gather(value_three, ('experts', 'context'), axis=1, tiled=True)  58.4 us
    dynamic_slice x8, local copies, waits for them, and re-layouts, key_visit(): lax.dynamic_slice_in_dim(grad_all, local_at, key_block_rows, 1)  53.3 us
    psum x1, blocking collectives, on_device(): lax.psum((grad_norm_attn, grad_w_query, grad_w_key, grad_w_value, grad_w_...  40.6 us
  transfers between devices with their start and end apart: 12, of which 6 were waited for; matrix products, arithmetic and copies ran while one was open for 44% of the time, Pallas kernels for 0%

commit v1 on v0

--- a/solution.py
+++ b/solution.py
@@ -2,7 +2,10 @@
 
 import jax
 import jax.numpy as jnp
+import numpy as np
 from jax import lax
+from jax.experimental import pallas as pl
+from jax.experimental.pallas import tpu as pltpu
 from jax.sharding import PartitionSpec as P
 
 MAXDIST = 128
@@ -399,7 +402,951 @@
     )
 
 
+MESH = pl.DeviceIdType.MESH
+BF = jnp.bfloat16
+F32 = jnp.float32
+VMEM = pltpu.VMEM
+ORDERS = (("x", "y", "l"), ("y", "l", "x"), ("l", "x", "y"))
+COLUMNS = ((0, 384), (384, 384), (768, 256))
+BIG = -1e30
+TILE = 256
+PLACES = 80
+SHARE = 704
+NT = (((1,), (1,)), ((), ()))
+TN = (((0,), (0,)), ((), ()))
+CUBE_SEMS = [pltpu.SemaphoreType.DMA((3, 8))] * 4
+
+
+def spot():
+    e = lax.axis_index("experts")
+    c = lax.axis_index("context")
+    return dict(k=lax.rem(e, 2), y=e // 2, x=lax.rem(c, 2), l=lax.rem(c // 2, 2), h=c // 4)
+
+
+def flip(b, names):
+    return {n: (1 - v if n in names else v) for n, v in b.items()}
+
+
+def device(b):
+    return {"experts": b["y"] * 2 + b["k"], "context": b["h"] * 4 + b["l"] * 2 + b["x"]}
+
+
+def row_of(b):
+    return b["y"] * 2 + b["k"]
+
+
+def col_of(b):
+    return b["l"] * 2 + b["x"]
+
+
+def slot_of(b):
+    return row_of(b) * 4 + col_of(b)
+
+
+def greet(peers):
+    barrier = pltpu.get_barrier_semaphore()
+    for peer in peers:
+        pl.semaphore_signal(barrier, inc=1, device_id=peer, device_id_type=MESH)
+    pl.semaphore_wait(barrier, len(peers))
+
+
+def cube_peers(b):
+    return [device(flip(b, [n])) for n in ("x", "y", "l", "k")]
+
+
+def cube_all(b):
+    peers = []
+    for step in range(1, 16):
+        s = lax.rem(slot_of(b) + step, 16)
+        peers.append({"experts": s // 4, "context": b["h"] * 4 + lax.rem(s, 4)})
+    return peers
+
+
+def world_all(b):
+    me = row_of(b) * 8 + b["h"] * 4 + col_of(b)
+    peers = []
+    for step in range(1, 32):
+        j = lax.rem(me + step, 32)
+        peers.append((j, {"experts": j // 8, "context": lax.rem(j, 8)}))
+    return me, peers
+
+
+def remote(src, dst, ssem, rsem, peer):
+    return pltpu.make_async_remote_copy(
+        src_ref=src, dst_ref=dst, send_sem=ssem, recv_sem=rsem, device_id=peer, device_id_type=MESH
+    )
+
+
+def names_of(order, t):
+    return [order[i] for i in range(3) if (t >> i) & 1]
+
+
+def gather_cube(b, view, ss, rs, cs, cr):
+    started = []
+    core = device(flip(b, ["k"]))
+
+    def link(p, t, i):
+        ref = view(flip(b, names_of(ORDERS[p], t)), p)
+        n = t | (1 << i)
+        cp = remote(ref, ref, ss.at[p, n], rs.at[p, n], device(flip(b, [ORDERS[p][i]])))
+        cp.start()
+        started.append(cp)
+
+    def across(p, t):
+        ref = view(flip(b, names_of(ORDERS[p], t)), p)
+        cp = remote(ref, ref, cs.at[p, t], cr.at[p, t], core)
+        cp.start()
+        started.append(cp)
+
+    for i in range(3):
+        for p in range(3):
+            link(p, 0, i)
+    for p in range(3):
+        across(p, 0)
+    for t in range(1, 8):
+        for p in range(3):
+            ref = view(flip(b, names_of(ORDERS[p], t)), p)
+            remote(ref, ref, ss.at[p, t], rs.at[p, t], core).wait_recv()
+            for i in range(t.bit_length(), 3):
+                link(p, t, i)
+            across(p, t)
+    for cp in started:
+        cp.wait_send()
+    for p in range(3):
+        for t in range(8):
+            ref = view(flip(b, names_of(ORDERS[p], t) + ["k"]), p)
+            remote(ref, ref, cs.at[p, t], cr.at[p, t], core).wait_recv()
+
+
+def eighth(b):
+    return b["y"] * 4 + b["l"] * 2 + b["x"]
+
+
+def scatter_cube(b, parts, acc, landing, ss, rs, cs, cr):
+    started = []
+    core = device(flip(b, ["k"]))
+    combos = [(y, l, x) for y in range(2) for l in range(2) for x in range(2)]
+    order = sorted(range(8), key=lambda t: -bin(t).count("1"))
+
+    def bits_t(t):
+        return flip(b, [n for i, n in enumerate(("x", "y", "l")) if (t >> i) & 1])
+
+    for t in order:
+        there = flip(bits_t(t), ["k"])
+        cp = remote(parts.at[slot_of(there)], acc.at[eighth(there)], cs.at[0, t], cr.at[0, t], core)
+        cp.start()
+        started.append(cp)
+    for t in order:
+        here = bits_t(t)
+        n = eighth(here)
+        remote(parts.at[slot_of(here)], acc.at[n], cs.at[0, t], cr.at[0, t], core).wait_recv()
+        acc[n] = (acc[n].astype(F32) + parts[slot_of(here)].astype(F32)).astype(BF)
+    for step in range(3):
+        rest = 2 - step
+        count = 1 << rest
+        for p in range(3):
+            c0, cn = COLUMNS[p]
+            first = ORDERS[p][step]
+            others = ORDERS[p][step + 1 :]
+            for t in range(count - 1, -1, -1):
+                there = flip(b, [first] + [others[i] for i in range(rest) if (t >> i) & 1])
+                n = count + t
+                cp = remote(
+                    acc.at[eighth(there), :, pl.ds(c0, cn)],
+                    landing.at[n, :, pl.ds(c0, cn)],
+                    ss.at[p, n],
+                    rs.at[p, n],
+                    device(flip(b, [first])),
+                )
+                cp.start()
+                started.append(cp)
+        for p in range(3):
+            c0, cn = COLUMNS[p]
+            others = ORDERS[p][step + 1 :]
+            for t in range(count - 1, -1, -1):
+                here = flip(b, [others[i] for i in range(rest) if (t >> i) & 1])
+                n = count + t
+                target = eighth(here)
+                ref = landing.at[n, :, pl.ds(c0, cn)]
+                remote(ref, ref, ss.at[p, n], rs.at[p, n], core).wait_recv()
+                acc[target, :, c0 : c0 + cn] = (
+                    acc[target, :, c0 : c0 + cn].astype(F32)
+                    + landing[n, :, c0 : c0 + cn].astype(F32)
+                ).astype(BF)
+    for cp in started:
+        cp.wait_send()
+
+
+def params(cid=None, mib=60):
+    if cid is None:
+        return pltpu.CompilerParams(vmem_limit_bytes=mib * 2**20)
+    return pltpu.CompilerParams(
+        collective_id=cid, has_side_effects=True, vmem_limit_bytes=mib * 2**20
+    )
+
+
+def call(body, outs, scratch, cid, *args, flops=0, data=0):
+    return pl.pallas_call(
+        body,
+        out_shape=outs,
+        in_specs=[pl.BlockSpec(memory_space=VMEM)] * len(args),
+        out_specs=[pl.BlockSpec(memory_space=VMEM)] * len(outs),
+        scratch_shapes=scratch,
+        compiler_params=params(cid),
+        cost_estimate=pl.CostEstimate(flops=flops, bytes_accessed=data, transcendentals=0),
+    )(*args)
+
+
+def shape(dims, kind=BF):
+    return jax.ShapeDtypeStruct(dims, kind)
+
+
+def gather_sequence(b, whole, staged, sems, hs, hr):
+    partner = device(flip(b, ["h"]))
+    mine = whole.at[row_of(b), b["h"], col_of(b)]
+    cp = remote(staged.at[1 - b["h"]], mine, hs, hr, partner)
+    cp.start()
+    whole[row_of(b), b["h"], col_of(b)] = staged[b["h"]]
+    theirs = whole.at[row_of(b), 1 - b["h"], col_of(b)]
+    remote(theirs, theirs, hs, hr, partner).wait_recv()
+
+    def view(v, p):
+        c0, cn = COLUMNS[p]
+        return whole.at[row_of(v), :, col_of(v), :, pl.ds(c0, cn)]
+
+    gather_cube(b, view, *sems)
+    cp.wait_send()
+
+
+def group_view(ref):
+    def view(v, p):
+        c0, cn = COLUMNS[p]
+        return ref.at[slot_of(v), :, pl.ds(c0, cn)]
+
+    return view
+
+
+def send_small(b, src, into, ss, rs):
+    copies = []
+    for step, peer in enumerate(cube_all(b)):
+        cp = remote(src, into.at[slot_of(b)], ss.at[step], rs.at[step], peer)
+        cp.start()
+        copies.append(cp)
+    return copies
+
+
+def wait_small(b, into, ss, rs, copies):
+    me = slot_of(b)
+    for step in range(15):
+        came = into.at[lax.rem(me + 15 - step, 16)]
+        remote(came, came, ss.at[step], rs.at[step], device(b)).wait_recv()
+    for cp in copies:
+        cp.wait_send()
+
+
+def inverse_rms(values):
+    return lax.rsqrt(jnp.mean(values * values, axis=-1, keepdims=True) + norm_epsilon)
+
+
+def first_body(tokens, cot, gain, picks, h1, dy, picks_all, staged, *sems):
+    b = spot()
+    greet([device(flip(b, ["h"]))] + cube_all(b))
+    copies = send_small(b, picks, picks_all, sems[10], sems[11])
+    picks_all[slot_of(b)] = picks[...]
+    for s in range(2):
+        rows = tokens[s].astype(F32)
+        staged[s] = (rows * inverse_rms(rows) * gain[...]).astype(BF)
+    gather_sequence(b, h1, staged, sems[0:4], sems[8], sems[9])
+    dy[slot_of(b)] = cot[...]
+    gather_cube(b, group_view(dy), *sems[4:8])
+    wait_small(b, picks_all, sems[10], sems[11], copies)
+
+
+def lane(shape_, dim=1):
+    return lax.broadcasted_iota(jnp.int32, shape_, dim)
+
+
+def near_tiles(row):
+    wide = jnp.broadcast_to(row, (TILE, 2 * TILE))
+    wide = pltpu.roll(wide, 0, 1, stride=1, stride_axis=0)
+    later = lax.broadcasted_iota(jnp.int32, (TILE, TILE), 0) > lane((TILE, TILE))
+    return [jnp.where(later, BIG, wide[:, :TILE]), wide[:, TILE:]]
+
+
+def pack_halves(rows):
+    n = rows.shape[0] // 64
+    four = rows.reshape(n, 2, 32, 128)
+    return jnp.where(
+        lax.broadcasted_iota(jnp.int32, (n, 32, 128), 2) < 64,
+        four[:, 0],
+        pltpu.roll(four[:, 1].reshape(n * 32, 128), 64, 1).reshape(n, 32, 128),
+    )
+
+
+def attend_body(length, h1, w3, dist, packed, out_t, qs, ks, vs, lse, strip, v_t, weights):
+    limit = length[0]
+    for i in range(8):
+        rows = slice(i * TILE, (i + 1) * TILE)
+        p = jnp.dot(h1[rows], w3[...], preferred_element_type=F32)
+        spot_lane = lane((TILE, 128))
+        where_at = lax.broadcasted_iota(jnp.int32, (TILE, 128), 0) + i * TILE
+        one = spot_lane == 64
+        qs[rows] = jnp.where(one, 1.0, p[:, :128] * 0.125).astype(BF)
+        ks[rows] = jnp.where(one & (where_at >= limit), BIG, p[:, 128:256]).astype(BF)
+        v = jnp.where(one, 1.0, p[:, 256:]).astype(BF)
+        vs[rows] = v
+        v_t[:, rows] = v.astype(F32).T.astype(BF)
+    near = near_tiles(dist[0:1])
+    for i in range(8):
+        cols = slice(i * TILE, (i + 1) * TILE)
+        q = qs[cols]
+        top = None
+        for j in range(i + 1):
+            rows = slice(j * TILE, (j + 1) * TILE)
+            s = lax.dot_general(ks[rows], q, NT, preferred_element_type=F32)
+            if i - j < 2:
+                s = s + near[i - j]
+            strip[rows] = s
+            m = jnp.max(s, axis=0, keepdims=True)
+            top = m if top is None else jnp.maximum(top, m)
+        for j in range(i + 1):
+            rows = slice(j * TILE, (j + 1) * TILE)
+            weights[rows] = jnp.exp(strip[rows] - top).astype(BF)
+        n = (i + 1) * TILE
+        o = jnp.dot(v_t[:, :n], weights[:n], preferred_element_type=F32)
+        total = o[64:65]
+        o = o / total
+        lse[:, cols] = jnp.broadcast_to(top + jnp.log(total), (8, TILE))
+        out_t[:, cols] = o[:64]
+        packed[4 * i : 4 * i + 4] = pack_halves(o.T).astype(BF)
+
+
+def unpack_halves(first, second):
+    a = first.astype(F32)
+    c = second.astype(F32)
+    left = lane((32, 128)) < 64
+    top = jnp.where(left, a, pltpu.roll(c, 64, 1))
+    bottom = jnp.where(left, pltpu.roll(a, 64, 1), c)
+    return top.astype(BF), bottom.astype(BF)
+
+
+def everyone(b, src, dst_at, ss, rs):
+    me, peers = world_all(b)
+    copies = []
+    for step, (j, peer) in enumerate(peers):
+        cp = remote(src.at[j], dst_at(me), ss.at[step], rs.at[step], peer)
+        cp.start()
+        copies.append(cp)
+    return me, copies
+
+
+def everyone_wait(b, me, dst_at, ss, rs, copies):
+    for step in range(31):
+        came = dst_at(lax.rem(me + 31 - step, 32))
+        remote(came, came, ss.at[step], rs.at[step], device(b)).wait_recv()
+    for cp in copies:
+        cp.wait_send()
+
+
+def middle_body(packed, tokens, w_out, gain, router3, middle, h2_all, gates_all, land, joined, gates, *sems):
+    b = spot()
+    greet([peer for _, peer in world_all(b)[1]])
+
+    def at(j):
+        return land.at[j]
+
+    me, copies = everyone(b, packed, at, sems[4], sems[5])
+    land[me] = packed[me]
+    everyone_wait(b, me, at, sems[4], sems[5], copies)
+    for s in range(2):
+        for pair in range(8):
+            first, second = 2 * pair, 2 * pair + 1
+            j0 = (first // 4) * 8 + s * 4 + first % 4
+            j1 = (second // 4) * 8 + s * 4 + second % 4
+            top, bottom = unpack_halves(land[j0], land[j1])
+            cols = slice(pair * 128, pair * 128 + 128)
+            joined[s * 64 : s * 64 + 32, cols] = top
+            joined[s * 64 + 32 : s * 64 + 64, cols] = bottom
+    x = tokens[...].astype(F32)
+    mid = x + jnp.dot(joined[...], w_out[...], preferred_element_type=F32)
+    middle[...] = mid
+    h2 = (mid * inverse_rms(mid) * gain[...]).astype(BF)
+    h2_all[slot_of(b)] = h2
+    gather_half = group_view(h2_all)
+    logits = jnp.dot(h2, router3[...], preferred_element_type=F32).T
+    logits = logits[0:8] + logits[8:16] + logits[16:24]
+    real = lax.broadcasted_iota(jnp.int32, (8, 128), 0) < 4
+    logits = jnp.where(real, logits, BIG)
+    g = jnp.exp(logits - jnp.max(logits, axis=0, keepdims=True))
+    gates[...] = g / jnp.sum(g, axis=0, keepdims=True)
+    small = send_small(b, gates, gates_all, sems[6], sems[7])
+    gates_all[slot_of(b)] = gates[...]
+    gather_cube(b, gather_half, *sems[0:4])
+    wait_small(b, gates_all, sems[6], sems[7], small)
+
+
+def expert_body(
+    h2, dy, gates, picks, wg, wu, wd, routed, dh2, dgates, gwg, gwu, gwd, rows, grad, dexp, weight, hid, dgs, dus, outs, drs, dws
+):
+    mine = lax.axis_index("experts")
+    mine_f = mine.astype(F32)
+    first = picks[:, 0, :]
+    second = picks[:, 1, :]
+    chosen = jnp.where((first == mine_f) | (second == mine_f), 1.0, 0.0)
+    earlier = jnp.where(
+        lax.broadcasted_iota(jnp.int32, (128, 128), 0) < lane((128, 128)), 1.0, 0.0
+    )
+    place = jnp.dot(chosen.astype(BF), earlier.astype(BF), preferred_element_type=F32)
+    place = jnp.where((chosen > 0.5) & (place < PLACES), place, -1.0)
+    place_t = jnp.concatenate([place, jnp.full((112, 128), -1.0, F32)], axis=0).T
+    level = lax.broadcasted_iota(jnp.int32, (PLACES, 128), 0).astype(F32)
+    level_t = lane((128, PLACES)).astype(F32)
+    is_mine = lax.broadcasted_iota(jnp.int32, (8, 128), 0) == mine
+    for m in range(16):
+        at = slice(m * PLACES, (m + 1) * PLACES)
+        hit = jnp.where(level == place[m : m + 1], 1.0, 0.0)
+        hit_low = hit.astype(BF)
+        rows[at] = jnp.dot(hit_low, h2[m], preferred_element_type=F32).astype(BF)
+        g = jnp.dot(hit_low, dy[m], preferred_element_type=F32)
+        gate_row = jnp.sum(jnp.where(is_mine, gates[m], 0.0), axis=0, keepdims=True)
+        w = jnp.sum(hit * gate_row, axis=1, keepdims=True)
+        grad[at] = g.astype(BF)
+        dexp[at] = (w * g).astype(BF)
+        weight[at] = jnp.broadcast_to(w, (PLACES, 128))
+    c0 = math.sqrt(2.0 / math.pi)
+    c1 = 0.044715
+    for i in range(5):
+        at = slice(i * TILE, (i + 1) * TILE)
+        r = rows[at]
+        gp = jnp.dot(r, wg[...], preferred_element_type=F32)
+        up = jnp.dot(r, wu[...], preferred_element_type=F32)
+        sq = gp * gp
+        th = jnp.tanh(c0 * gp * (1.0 + c1 * sq))
+        half = 0.5 * (1.0 + th)
+        act = gp * half
+        slope = half + 0.5 * gp * (1.0 - th * th) * (c0 * (1.0 + 3.0 * c1 * sq))
+        h = (act * up).astype(BF)
+        hid[at] = h
+        o = jnp.dot(h, wd[...], preferred_element_type=F32)
+        w = weight[at, 0:1]
+        outs[at] = (w * o).astype(BF)
+        dws[at] = jnp.broadcast_to(
+            jnp.sum(grad[at].astype(F32) * o, axis=1, keepdims=True), (TILE, 128)
+        )
+        dh = lax.dot_general(dexp[at], wd[...], NT, preferred_element_type=F32)
+        dg = (dh * up * slope).astype(BF)
+        du = (dh * act).astype(BF)
+        dgs[at] = dg
+        dus[at] = du
+        drs[at] = (
+            lax.dot_general(dg, wg[...], NT, preferred_element_type=F32)
+            + lax.dot_general(du, wu[...], NT, preferred_element_type=F32)
+        ).astype(BF)
+    for m in range(16):
+        at = slice(m * PLACES, (m + 1) * PLACES)
+        back = jnp.where(place_t[:, m : m + 1] == level_t, 1.0, 0.0).astype(BF)
+        routed[m] = jnp.dot(back, outs[at], preferred_element_type=F32).astype(BF)
+        dh2[m] = jnp.dot(back, drs[at], preferred_element_type=F32).astype(BF)
+        hit = jnp.where(level == place[m : m + 1], 1.0, 0.0)
+        dgates[m] = jnp.broadcast_to(
+            jnp.sum(hit * dws[at], axis=0, keepdims=True), (8, 128)
+        )
+    gwd[...] = lax.dot_general(hid[...], dexp[...], TN, preferred_element_type=F32).astype(BF)
+    gwg[...] = lax.dot_general(rows[...], dgs[...], TN, preferred_element_type=F32).astype(BF)
+    gwu[...] = lax.dot_general(rows[...], dus[...], TN, preferred_element_type=F32).astype(BF)
+
+
+def norm_back_rows(values, gain, grad_in):
+    inverse = inverse_rms(values)
+    normed = values * inverse
+    scaled = grad_in * gain
+    out = inverse * (scaled - normed * jnp.mean(scaled * normed, axis=-1, keepdims=True))
+    return out, jnp.sum(grad_in * normed, axis=0, keepdims=True)
+
+
+def back_body(
+    dh2, dgates, gates, cot, keep, middle, gain, router_t, h2_all, dm_all, dmid, smalls, acc, landing, dg_all, staged, *sems
+):
+    b = spot()
+    greet([device(flip(b, ["h"]))] + cube_all(b))
+    me = slot_of(b)
+    copies = []
+    for step, peer in enumerate(cube_all(b)):
+        s = lax.rem(me + step + 1, 16)
+        cp = remote(dgates.at[s], dg_all.at[me], sems[10].at[step], sems[11].at[step], peer)
+        cp.start()
+        copies.append(cp)
+    dg_all[me] = dgates[me]
+    scatter_cube(b, dh2, acc, landing, *sems[0:4])
+    wait_small(b, dg_all, sems[10], sems[11], copies)
+    level = lax.broadcasted_iota(jnp.int32, (8, 128), 0)
+    dg = jnp.zeros((8, 128), F32)
+    for e in range(4):
+        total = dg_all[4 * e] + dg_all[4 * e + 1] + dg_all[4 * e + 2] + dg_all[4 * e + 3]
+        dg = jnp.where(level == e, total, dg)
+    g = gates[me]
+    dl_t = g * (dg - jnp.sum(g * dg, axis=0, keepdims=True))
+    dl = jnp.concatenate([dl_t, jnp.zeros((120, 128), F32)], axis=0).T
+    d_h2 = acc[eighth(b)].astype(F32)
+    for e in range(4):
+        d_h2 = d_h2 + dl[:, e : e + 1] * router_t[e : e + 1]
+    high = dl_t.astype(BF)
+    rest = (dl_t - high.astype(F32)).astype(BF)
+    h2 = h2_all[me]
+    smalls[0:8] = jnp.dot(high, h2, preferred_element_type=F32) + jnp.dot(
+        rest, h2, preferred_element_type=F32
+    )
+    grad_mid, grad_gain = norm_back_rows(middle[...], gain[...], d_h2)
+    smalls[4:5] = grad_gain
+    d_mid = cot[...].astype(F32) * keep[...] + grad_mid
+    dmid[...] = d_mid
+    staged[0] = d_mid[:64].astype(BF)
+    staged[1] = d_mid[64:].astype(BF)
+    gather_sequence(b, dm_all, staged, sems[4:8], sems[8], sems[9])
+
+
+def attend_back_body(
+    h1, dm, w_o, qs, ks, vs, out_t, lse, dist, packed, grads, sums, dos, k_t, delta, p_buf, s_buf, dq_t, dk, dv, near0, near1, left
+):
+    for i in range(8):
+        rows = slice(i * TILE, (i + 1) * TILE)
+        d = lax.dot_general(dm[rows], w_o[...], NT, preferred_element_type=F32).astype(BF)
+        dos[rows] = d
+        delta[:, rows] = jnp.broadcast_to(
+            jnp.sum(d.astype(F32).T[:64] * out_t[:, rows], axis=0, keepdims=True), (8, TILE)
+        )
+        kt = ks[rows].astype(F32).T
+        k_t[:, rows] = jnp.where(
+            lax.broadcasted_iota(jnp.int32, (128, TILE), 0) == 64, 1.0, kt
+        ).astype(BF)
+    near = near_tiles(dist[0:1])
+    near0[...] = jnp.zeros_like(near0)
+    near1[...] = jnp.zeros_like(near1)
+    for i in range(8):
+        cols = slice(i * TILE, (i + 1) * TILE)
+        q = qs[cols]
+        do = dos[cols]
+        level = lse[0:1, cols]
+        dl = delta[0:1, cols]
+        for j in range(i + 1):
+            rows = slice(j * TILE, (j + 1) * TILE)
+            s = lax.dot_general(ks[rows], q, NT, preferred_element_type=F32)
+            if i - j < 2:
+                s = s + near[i - j]
+            p = jnp.exp(s - level)
+            dp = lax.dot_general(vs[rows], do, NT, preferred_element_type=F32)
+            ds = (p * (dp - dl)).astype(BF)
+            p_buf[rows] = p.astype(BF)
+            s_buf[rows] = ds
+            if i == j:
+                near0[...] += ds.astype(F32)
+            if i - j == 1:
+                near1[...] += ds.astype(F32)
+        n = (i + 1) * TILE
+        dq_t[:, cols] = jnp.dot(k_t[:, :n], s_buf[:n], preferred_element_type=F32)
+        new_v = jnp.dot(p_buf[:n], do, preferred_element_type=F32)
+        new_k = jnp.dot(s_buf[:n], q, preferred_element_type=F32)
+        if i > 0:
+            dv[: n - TILE] += new_v[: n - TILE]
+            dk[: n - TILE] += new_k[: n - TILE]
+        dv[n - TILE : n] = new_v[n - TILE :]
+        dk[n - TILE : n] = new_k[n - TILE :]
+    total = jnp.sum(dq_t[64:65, :].reshape(1, 16, 128), axis=1)
+    skew = jnp.concatenate([near0[...], near1[...]], axis=1)
+    level_u = lax.broadcasted_iota(jnp.int32, (TILE, 2 * TILE), 0)
+    for bit in range(8):
+        moved = pltpu.roll(skew, 2 * TILE - (1 << bit), 1)
+        skew = jnp.where((level_u // (1 << bit)) % 2 == 1, moved, skew)
+    sums[0:1] = jnp.sum(skew, axis=0, keepdims=True)
+    sums[1:2] = jnp.concatenate([total, jnp.zeros((1, 384), F32)], axis=1)
+    for i in range(8):
+        rows = slice(i * TILE, (i + 1) * TILE)
+        dq = dq_t[:, rows] * 0.125
+        vk = jnp.where(lane((TILE, 128)) < 64, dv[rows], pltpu.roll(dk[rows], 64, 1)).T
+        left[0:64, rows] = dq[:64].astype(BF)
+        left[64:128, rows] = vk[64:128].astype(BF)
+        left[128:192, rows] = vk[0:64].astype(BF)
+        left[192:256, rows] = out_t[:, rows].astype(BF)
+        blocks = slice(4 * i, 4 * i + 4)
+        packed[blocks, 0:32] = pack_halves(dq.T).astype(BF)
+        packed[blocks, 32:64] = pack_halves(dk[rows]).astype(BF)
+        packed[blocks, 64:96] = pack_halves(dv[rows]).astype(BF)
+    qkv = jnp.dot(left[0:192], h1[...], preferred_element_type=F32).astype(BF)
+    grads[0] = qkv[0:128]
+    grads[1, 0:64] = qkv[128:192]
+    grads[1, 64:128] = jnp.dot(left[192:256], dm[...], preferred_element_type=F32).astype(BF)
+
+
+def last_body(
+    packed, grads, tokens, dmid, gain, wq, wk, wv, part, dtokens, whole, smalls, land, other, joined, inbox, *sems
+):
+    b = spot()
+    greet([peer for _, peer in world_all(b)[1]])
+    partner = device(flip(b, ["h"]))
+    h = b["h"]
+    trade = remote(grads.at[1 - h], other, sems[8].at[0], sems[9].at[0], partner)
+    trade.start()
+
+    def at(j):
+        return land.at[j]
+
+    me, copies = everyone(b, packed, at, sems[10], sems[11])
+    land[me] = packed[me]
+    trade.wait()
+    me_slot = slot_of(b)
+    whole[h, me_slot] = (grads[h].astype(F32) + other[...].astype(F32)).astype(BF)
+    share = remote(
+        whole.at[h, me_slot], whole.at[h, me_slot], sems[8].at[1], sems[9].at[1], partner
+    )
+    share.start()
+
+    def view_of(side):
+        def view(v, p):
+            c0, cn = COLUMNS[p]
+            return whole.at[side, slot_of(v), :, pl.ds(c0, cn)]
+
+        return view
+
+    gather_cube(b, view_of(h), *sems[0:4])
+    theirs = whole.at[1 - h, me_slot]
+    share.wait_send()
+    remote(theirs, theirs, sems[8].at[1], sems[9].at[1], partner).wait_recv()
+    gather_cube(b, view_of(1 - h), *sems[4:8])
+    everyone_wait(b, me, at, sems[10], sems[11], copies)
+    for kind in range(3):
+        for s in range(2):
+            for pair in range(8):
+                first, second = 2 * pair, 2 * pair + 1
+                j0 = (first // 4) * 8 + s * 4 + first % 4
+                j1 = (second // 4) * 8 + s * 4 + second % 4
+                span = slice(kind * 32, kind * 32 + 32)
+                top, bottom = unpack_halves(land[j0, span], land[j1, span])
+                cols = slice(pair * 128, pair * 128 + 128)
+                joined[kind, s * 64 : s * 64 + 32, cols] = top
+                joined[kind, s * 64 + 32 : s * 64 + 64, cols] = bottom
+    d_h1 = (
+        lax.dot_general(joined[0], wq[...], NT, preferred_element_type=F32)
+        + lax.dot_general(joined[1], wk[...], NT, preferred_element_type=F32)
+        + lax.dot_general(joined[2], wv[...], NT, preferred_element_type=F32)
+    )
+    grad_in, grad_gain = norm_back_rows(tokens[...].astype(F32), gain[...], d_h1)
+    dtokens[...] = dmid[...] + grad_in
+    smalls[...] = part[...]
+    smalls[5:6] = grad_gain
+    for step, name in enumerate(("k", "x", "y", "l", "h")):
+        cp = remote(
+            smalls, inbox.at[step], sems[12].at[step], sems[13].at[step], device(flip(b, [name]))
+        )
+        cp.start()
+        cp.wait()
+        smalls[...] = smalls[...] + inbox[step]
+
+
+def routed_body(routed, middle, keep, gwg, gwu, gwd, result, down, wide, acc, landing, inbox_w, inbox_d, half, *sems):
+    b = spot()
+    h = b["h"]
+    col = col_of(b)
+    partner = device(flip(b, ["h"]))
+    around = []
+    for names in (["x"], ["l"], ["x", "l"]):
+        around.append(flip(b, names))
+    greet([partner] + cube_peers(b) + [device(around[2])])
+    trades = [
+        remote(gwg.at[1 - h], inbox_w.at[0], sems[4].at[0], sems[5].at[0], partner),
+        remote(gwu.at[1 - h], inbox_w.at[1], sems[4].at[1], sems[5].at[1], partner),
+        remote(gwd.at[1 - h], inbox_d, sems[4].at[2], sems[5].at[2], partner),
+    ]
+    for cp in trades:
+        cp.start()
+    scatter_cube(b, routed, acc, landing, *sems[0:4])
+    result[...] = (
+        (middle[...] + acc[eighth(b)].astype(F32)) * keep[...]
+    ).astype(BF)
+    started = []
+    for n, g in enumerate((gwg, gwu)):
+        trades[n].wait()
+        half[n] = (g[h].astype(F32) + inbox_w[n].astype(F32)).astype(BF)
+        for i, there in enumerate(around):
+            cp = remote(
+                half.at[n, col_of(there)],
+                wide.at[n, col],
+                sems[6].at[3 * n + i],
+                sems[7].at[3 * n + i],
+                device(there),
+            )
+            cp.start()
+            started.append(cp)
+        wide[n, col] = half[n, col]
+    trades[2].wait()
+    down[...] = gwd[h].astype(F32) + inbox_d[...].astype(F32)
+    for n in range(2):
+        for i, there in enumerate(around):
+            ref = wide.at[n, col_of(there)]
+            remote(ref, ref, sems[6].at[3 * n + i], sems[7].at[3 * n + i], device(there)).wait_recv()
+    for cp in started:
+        cp.wait_send()
+
+
+def distance_buckets():
+    table = []
+    for distance in range(2 * TILE):
+        table.append(bucket_of(distance, 32, MAXDIST))
+    return np.array(table, np.int32)
+
+
+def on_device_fast(
+    tokens,
+    lengths,
+    expert_index,
+    cotangent,
+    norm_attn,
+    w_query,
+    w_key,
+    w_value,
+    w_out,
+    rel_bias,
+    norm_ffn,
+    router,
+    w_gate,
+    w_up,
+    w_down,
+):
+    dma = pltpu.SemaphoreType.DMA
+    b = spot()
+    head = slot_of(b)
+    col = col_of(b)
+    device_at = lax.axis_index(("experts", "context"))
+    positions = device_at * 64 + jnp.arange(64, dtype=jnp.int32)
+    live = positions[None, :] < lengths[:, None]
+    keep = live.reshape(128, 1).astype(F32)
+    picks = jnp.where(live[:, :, None], expert_index, -1).astype(F32).reshape(128, 2).T
+    picks = jnp.concatenate([picks, jnp.zeros((6, 128), F32)], axis=0)
+    gain_attn = norm_attn.reshape(1, 1024)
+    gain_ffn = norm_ffn.reshape(1, 1024)
+    flat = tokens.reshape(128, 1024)
+    cot = cotangent.reshape(128, 1024)
+
+    def head_columns(w):
+        return jnp.pad(lax.dynamic_slice_in_dim(w, head * 64, 64, 1), ((0, 0), (0, 64)))
+
+    w3 = jnp.concatenate([head_columns(w_query), head_columns(w_key), head_columns(w_value)], axis=1)
+    w_o = jnp.pad(lax.dynamic_slice_in_dim(w_out, head * 64, 64, 0), ((0, 64), (0, 0)))
+    buckets = distance_buckets()
+    onehot = np.zeros((2 * TILE, 32), np.float32)
+    onehot[np.arange(2 * TILE), buckets] = 1.0
+    bias = lax.dynamic_slice_in_dim(rel_bias, head, 1, 1)[:, 0]
+    by_distance = jnp.dot(jnp.asarray(onehot), bias - bias[31], precision=highest)
+    dist = jnp.broadcast_to(by_distance[None], (8, 2 * TILE))
+    mine = lax.dynamic_slice_in_dim(lengths, b["h"], 1, 0)
+
+    def columns_share(w):
+        return lax.dynamic_index_in_dim(
+            w[0].reshape(1024, 2, 4, 352), col, 2, keepdims=False
+        ).reshape(1024, SHARE)
+
+    wg = columns_share(w_gate)
+    wu = columns_share(w_up)
+    wd = lax.dynamic_index_in_dim(
+        w_down[0].reshape(2, 4, 352, 1024), col, 1, keepdims=False
+    ).reshape(SHARE, 1024)
+    high = router.astype(BF)
+    rest = router - high.astype(F32)
+    mid = rest.astype(BF)
+    lo = (rest - mid.astype(F32)).astype(BF)
+    router3 = jnp.concatenate(
+        [jnp.pad(r, ((0, 0), (0, 4))) for r in (high, mid, lo)] + [jnp.zeros((1024, 104), BF)], axis=1
+    )
+    router_t = jnp.pad(router.T, ((0, 4), (0, 0)))
+
+    h1, dy_all, picks_all = call(
+        first_body,
+        [shape((4, 2, 4, 64, 1024)), shape((16, 128, 1024)), shape((16, 8, 128), F32)],
+        [VMEM((2, 64, 1024), BF)] + CUBE_SEMS + CUBE_SEMS + [dma(()), dma(()), dma((15,)), dma((15,))],
+        1,
+        tokens,
+        cot,
+        gain_attn,
+        picks,
+    )
+    h1 = h1.reshape(2048, 1024)
+    packed, out_t, qs, ks, vs, lse = pl.pallas_call(
+        attend_body,
+        out_shape=[
+            shape((32, 32, 128)),
+            shape((64, 2048), F32),
+            shape((2048, 128)),
+            shape((2048, 128)),
+            shape((2048, 128)),
+            shape((8, 2048), F32),
+        ],
+        in_specs=[pl.BlockSpec(memory_space=pltpu.SMEM)] + [pl.BlockSpec(memory_space=VMEM)] * 3,
+        out_specs=[pl.BlockSpec(memory_space=VMEM)] * 6,
+        scratch_shapes=[VMEM((2048, TILE), F32), VMEM((128, 2048), BF), VMEM((2048, TILE), BF)],
+        compiler_params=params(),
+    )(mine, h1, w3, dist)
+    middle, h2_all, gates_all = call(
+        middle_body,
+        [shape((128, 1024), F32), shape((16, 128, 1024)), shape((16, 8, 128), F32)],
+        [VMEM((32, 32, 128), BF), VMEM((128, 1024), BF), VMEM((8, 128), F32)]
+        + CUBE_SEMS
+        + [dma((31,)), dma((31,)), dma((15,)), dma((15,))],
+        2,
+        packed,
+        flat,
+        w_out,
+        gain_ffn,
+        router3,
+    )
+    routed, dh2, dgates, gwg, gwu, gwd = call(
+        expert_body,
+        [
+            shape((16, 128, 1024)),
+            shape((16, 128, 1024)),
+            shape((16, 8, 128), F32),
+            shape((1024, SHARE)),
+            shape((1024, SHARE)),
+            shape((SHARE, 1024)),
+        ],
+        [VMEM((1280, 1024), BF)] * 3
+        + [VMEM((1280, 128), F32)]
+        + [VMEM((1280, SHARE), BF)] * 3
+        + [VMEM((1280, 1024), BF)] * 2
+        + [VMEM((1280, 128), F32)],
+        None,
+        h2_all,
+        dy_all,
+        gates_all,
+        picks_all,
+        wg,
+        wu,
+        wd,
+    )
+    dm_all, dmid, smalls = call(
+        back_body,
+        [shape((4, 2, 4, 64, 1024)), shape((128, 1024), F32), shape((8, 1024), F32)],
+        [
+            VMEM((8, 128, 1024), BF),
+            VMEM((8, 128, 1024), BF),
+            VMEM((16, 8, 128), F32),
+            VMEM((2, 64, 1024), BF),
+        ]
+        + CUBE_SEMS
+        + CUBE_SEMS
+        + [dma(()), dma(()), dma((15,)), dma((15,))],
+        3,
+        dh2,
+        dgates,
+        gates_all,
+        cot,
+        keep,
+        middle,
+        gain_ffn,
+        router_t,
+        h2_all,
+    )
+    packed_back, grads, sums = call(
+        attend_back_body,
+        [shape((32, 96, 128)), shape((2, 128, 1024)), shape((8, 512), F32)],
+        [
+            VMEM((2048, 128), BF),
+            VMEM((128, 2048), BF),
+            VMEM((8, 2048), F32),
+            VMEM((2048, TILE), BF),
+            VMEM((2048, TILE), BF),
+            VMEM((128, 2048), F32),
+            VMEM((2048, 128), F32),
+            VMEM((2048, 128), F32),
+            VMEM((TILE, TILE), F32),
+            VMEM((TILE, TILE), F32),
+            VMEM((256, 2048), BF),
+        ],
+        None,
+        h1,
+        dm_all.reshape(2048, 1024),
+        w_o,
+        qs,
+        ks,
+        vs,
+        out_t,
+        lse,
+        dist,
+    )
+    table = jnp.dot(sums[0], jnp.asarray(onehot), precision=highest)
+    table = table.at[31].set(jnp.sum(sums[1]) - jnp.sum(table[:31]))
+    row = lax.dynamic_update_slice_in_dim(jnp.zeros((1024,), F32), table, head * 32, 0)
+    smalls = jnp.concatenate([smalls[:6], row[None], jnp.zeros((1, 1024), F32)], axis=0)
+    dtokens, whole, smalls = call(
+        last_body,
+        [shape((128, 1024), F32), shape((2, 16, 128, 1024)), shape((8, 1024), F32)],
+        [
+            VMEM((32, 96, 128), BF),
+            VMEM((128, 1024), BF),
+            VMEM((3, 128, 1024), BF),
+            VMEM((5, 8, 1024), F32),
+        ]
+        + CUBE_SEMS
+        + CUBE_SEMS
+        + [dma((2,)), dma((2,)), dma((31,)), dma((31,)), dma((5,)), dma((5,))],
+        4,
+        packed_back,
+        grads,
+        flat,
+        dmid,
+        gain_attn,
+        w_query,
+        w_key,
+        w_value,
+        smalls,
+    )
+    result, down, wide = call(
+        routed_body,
+        [shape((128, 1024)), shape((352, 1024), F32), shape((2, 4, 128, SHARE))],
+        [
+            VMEM((8, 128, 1024), BF),
+            VMEM((8, 128, 1024), BF),
+            VMEM((2, 4, 128, SHARE), BF),
+            VMEM((352, 1024), BF),
+            VMEM((2, 4, 128, SHARE), BF),
+        ]
+        + CUBE_SEMS
+        + [dma((3,)), dma((3,)), dma((6,)), dma((6,))],
+        5,
+        routed,
+        middle,
+        keep,
+        gwg.reshape(2, 4, 128, SHARE),
+        gwu.reshape(2, 4, 128, SHARE),
+        gwd.reshape(2, 352, 1024),
+    )
+
+    def widen(w):
+        return (
+            w.reshape(4, 128, 2, 352).transpose(1, 2, 0, 3).reshape(1, 128, 2816).astype(F32)
+        )
+
+    def dense(rows):
+        return rows.reshape(1024, 1024).astype(F32)
+
+    return (
+        result.reshape(2, 64, 1024),
+        dtokens.reshape(2, 64, 1024),
+        smalls[5],
+        dense(whole[0, :, 0:64]).T,
+        dense(whole[0, :, 64:128]).T,
+        dense(whole[1, :, 0:64]).T,
+        dense(whole[1, :, 64:128]),
+        smalls[6, :512].reshape(16, 32).T,
+        smalls[4],
+        smalls[0:4].T,
+        widen(wide[0]),
+        widen(wide[1]),
+        down[None],
+    )
+
+
 def solution(mesh):
+    sizes = dict(mesh.shape)
+    fits = sizes == {"experts": 4, "context": 8}
     placed = (
         P(None, ("experts", "context"), None),
         P(),
@@ -418,7 +1365,7 @@
         P("experts", None, None),
     )
     return jax.shard_map(
-        on_device,
+        on_device_fast if fits else on_device,
         mesh=mesh,
         in_specs=placed,
         out_specs=(

time: 1240 us -> 530 us (0.43)
  Pallas kernels: 0 us -> 429 us
  waiting for transfers between devices: 366 us -> 0 us
  matrix products: 252 us -> 1.89 us
  blocking collectives: 247 us -> 0 us
  local copies, waits for them, and re-layouts: 261 us -> 67.5 us
  other arithmetic: 61 us -> 19.8 us
  starting transfers between devices: 17.6 us -> 0 us
  between operations: 15.3 us -> 2.67 us
    pallas_call x0 -> x8, Pallas kernels: none -> 429 us  [the longest x7 418 us: call(): pl.pallas_call(body, out_shape=outs, in_specs=[pl.BlockSpec(memory_space=...]
    dot_general x78 -> x2, matrix products: 252 us -> 1.89 us  [the longest x1 0.95 us: on_device_fast(): jnp.dot(jnp.asarray(onehot), bias - bias[31], precision=highest)]
    psum x1 -> x0, waiting for transfers between devices: 218 us -> none  [on_device(): lax.psum((grad_norm_attn, grad_w_query, grad_w_key, grad_w_value, grad_w_...]
    all_gather x2 -> x0, blocking collectives: 206 us -> none  [the longest x1 110 us: on_device(): lax.all_gather(delta, ('experts', 'context'), axis=1, tiled=True)]
    all_gather x4 -> x0, waiting for transfers between devices: 130 us -> none  [the longest x1 71.2 us: on_device(): lax.all_gather(key_three, ('experts', 'context'), axis=1, tiled=True)]
    dynamic_slice x36 -> x7, local copies, waits for them, and re-layouts: 117 us -> 8.51 us  [the longest x1 2.57 us: on_device_fast(): lax.dynamic_index_in_dim(w_down[0].reshape(2, 4, 352, 1024), col, 1, keep...]
    unnamed x147 -> x27, local copies, waits for them, and re-layouts: 90.3 us -> 23.7 us
    psum x1 -> x0, blocking collectives: 40.6 us -> none  [on_device(): lax.psum((grad_norm_attn, grad_w_query, grad_w_key, grad_w_value, grad_w_...]
  transfers between devices with their start and end apart: 12 -> 0, of which waited for: 6 -> 0; matrix products, arithmetic and copies ran while one was open for 44% -> 0% of each run, Pallas kernels for 0% -> 0%
where the time goes in v1:
time: 530 us; the launch traced here: 521 us
  Pallas kernels  429 us (81%)
  local copies, waits for them, and re-layouts  67.5 us (13%)
  other arithmetic  19.8 us (4%)
    pallas_call x7, Pallas kernels, call(): pl.pallas_call(body, out_shape=outs, in_specs=[pl.BlockSpec(memory_space=...  418 us
    unnamed x27, local copies, waits for them, and re-layouts  23.7 us
    pallas_call x1, Pallas kernels, on_device_fast(): pl.pallas_call(attend_body, out_shape=[shape((32, 32, 128)), shape((64, 2...  11 us

profile of v1, /device:TPU:0, one launch (start us, length us, event | category | flops | bytes accessed | tf_op | source)
XLA Modules:
  0.0 520.6 jit_solution(10446422783009792232)
XLA Ops:
  7.7 55.1 %shard_map.255 = (bf16[4,2,4,64,1024]{4,3,2,1,0:T(8,128)(2,1)}, bf16[16,128,1024]{2,1,0:T(8,128)(2,1)}, f32[16,8,128]{2,1,0:T(8,128)}) custom-call(bf16[2,64,1024]{2,1,0:T(8,128)(2,1)} %tokens.1, bf16[128,1024]{1,0:T(8,128)(2,1)} %bitcast.85, f32[1,1024]{1,0:T(1,128)} %bitcast.94, f32[8,128]{1,0:T(8,128)} %concatenate.14.picks), custom_call_target="tpu_custom_call" | custom-call | tf_op jit(solution)/shard_map/pallas_call | solution.py:589
  62.8 11.0 %shard_map.256 = (bf16[32,32,128]{2,1,0:T(8,128)(2,1)}, f32[64,2048]{1,0:T(8,128)}, bf16[2048,128]{1,0:T(8,128)(2,1)}, bf16[2048,128]{1,0:T(8,128)(2,1)}, bf16[2048,128]{1,0:T(8,128)(2,1)}, /*index=5*/f32[8,2048]{1,0:T(8,128)}) custom-call(s32[1]{0:T(128)} %dynamic_slice.29.length, bf16[2048,1024]{1,0:T(8,128)(2,1)} %bitcast.64, ...), custom_call_target="tpu_custom_call" | custom-call | tf_op jit(solution)/shard_map/pallas_call | solution.py:1172
  75.6 34.7 %shard_map.257 = (f32[128,1024]{1,0:T(8,128)}, bf16[16,128,1024]{2,1,0:T(8,128)(2,1)}, f32[16,8,128]{2,1,0:T(8,128)}) custom-call(bf16[32,32,128]{2,1,0:T(8,128)(2,1)} %get-tuple-element.56.packed, bf16[128,1024]{1,0:T(8,128)(2,1)} %bitcast.79, bf16[1024,1024]{1,0:T(8,128)(2,1)} %w_out.1, f32[1,1024]{1,0:T(1,128)} %bitcast.92, bf16[1024,128]{1,0:T(8,128)(2,1)} %fusion.12.router3), custom_call_target="tpu_custom_call" | custom-call | tf_op jit(solution)/shard_map/pallas_call | solution.py:589
  110.3 8.7 %copy.72 = bf16[1,1024,2816]{1,2,0:T(8,128)(2,1)} copy(bf16[1,1024,2816]{2,1,0:T(8,128)(2,1)} %param.31) | data formatting | bytes 11534336 | tf_op args[13]
  119.0 8.4 %copy.71 = bf16[1,1024,2816]{1,2,0:T(8,128)(2,1)} copy(bf16[1,1024,2816]{2,1,0:T(8,128)(2,1)} %param.30) | data formatting | bytes 11534336 | tf_op args[12]
  127.3 2.1 constant_dynamic-slice_fusion.2
  129.4 1.6 copy.74.wg
  132.5 2.6 constant_dynamic-slice_fusion.1
  135.1 29.4 %shard_map.258 = (bf16[16,128,1024]{2,1,0:T(8,128)(2,1)}, bf16[16,128,1024]{2,1,0:T(8,128)(2,1)}, f32[16,8,128]{2,1,0:T(8,128)}, bf16[1024,704]{1,0:T(8,128)(2,1...) custom-call(bf16[16,128,1024]{2,1,0:T(8,128)(2,1)} %get-tuple-element.57.h2.h2_all, ...), custom_call_target="tpu_custom_call" | custom-call | tf_op jit(solution)/shard_map/pallas_call | solution.py:589
  165.9 57.9 %shard_map.260 = (bf16[4,2,4,64,1024]{4,3,2,1,0:T(8,128)(2,1)}, f32[128,1024]{1,0:T(8,128)}, f32[8,1024]{1,0:T(8,128)}) custom-call(bf16[16,128,1024]{2,1,0:T(8,128)(2,1)} %get-tuple-element.67.dh2, f32[16,8,128]{2,1,0:T(8,128)} %get-tuple-element.68.dgates, f32[16,8,128]{2,1,0:T(8,128)} %get-tuple-element.59.gates, bf16[128,1024]{1,0:T(8,128)(2,1)} %bitcast.86, ...), custom_call_target="tpu_custom_call" | custom-call | tf_op jit(solution)/shard_map/pallas_call | solution.py:589
  225.4 13.8 %shard_map.261 = (bf16[32,96,128]{2,1,0:T(8,128)(2,1)}, bf16[2,128,1024]{2,1,0:T(8,128)(2,1)}, f32[8,512]{1,0:T(8,128)}) custom-call(bf16[2048,1024]{1,0:T(8,128)(2,1)} %bitcast.65, bf16[2048,1024]{1,0:T(8,128)(2,1)} %bitcast.78, bf16[128,1024]{1,0:T(8,128)(2,1)} %pad.38.w_o, bf16[2048,128]{1,0:T(8,128)(2,1)} %get-tuple-element.70.qs, ...), custom_call_target="tpu_custom_call" | custom-call | tf_op jit(solution)/shard_map/pallas_call | solution.py:589
  244.6 92.3 %shard_map.262 = (f32[128,1024]{1,0:T(8,128)}, bf16[2,16,128,1024]{3,2,1,0:T(8,128)(2,1)}, f32[8,1024]{1,0:T(8,128)}) custom-call(bf16[32,96,128]{2,1,0:T(8,128)(2,1)} %get-tuple-element.75.packed, bf16[2,128,1024]{2,1,0:T(8,128)(2,1)} %get-tuple-element.76.grads, bf16[128,1024]{1,0:T(8,128)(2,1)} %bitcast.80, f32[128,1024]{1,0:T(8,128)} %get-tuple-element.77.dmid, ...), custom_call_target="tpu_custom_call" | custom-call | tf_op jit(solution)/shard_map/pallas_call | solution.py:589
  337.0 5.4 %fusion.20 = (bf16[1,16,64,1024]{3,2,1,0:T(8,128)(2,1)S(1)}, bf16[1,16,64,1024]{3,2,1,0:T(8,128)(2,1)}, bf16[1,16,64,1024]{3,2,1,0:T(8,128)(2,1)}, bf16[1,16,64,1024]{3,2,1,0:T(8,128)(2,1)S(1)}) fusion(bf16[2,16,128,1024]{3,2,1,0:T(8,128)(2,1)} %get-tuple-element.82), kind=kLoop, calls=%fused_computation.54 | loop fusion | bytes 16777216 | tf_op jit(solution)/shard_map/slice | solution.py:1337
  342.4 2.6 bitcast_convert_fusion.3
  345.0 5.3 %copy.78 = f32[1024,1024]{0,1:T(8,128)} copy(f32[1024,1024]{1,0:T(8,128)} %bitcast_convert_fusion.3) | data formatting | bytes 8388608 | tf_op jit(solution)/shard_map/transpose | solution.py:1334
  350.4 4.1 bitcast_convert_fusion.2
  354.4 5.3 %copy.79 = f32[1024,1024]{0,1:T(8,128)} copy(f32[1024,1024]{1,0:T(8,128)} %bitcast_convert_fusion.2) | data formatting | bytes 8388608 | tf_op jit(solution)/shard_map/transpose | solution.py:1335
  359.8 4.1 bitcast_convert_fusion.1
  363.8 5.3 %copy.80 = f32[1024,1024]{0,1:T(8,128)} copy(f32[1024,1024]{1,0:T(8,128)} %bitcast_convert_fusion.1) | data formatting | bytes 8388608 | tf_op jit(solution)/shard_map/transpose | solution.py:1336
  369.2 2.6 bitcast_convert_fusion
  373.7 134.5 %shard_map.259 = (bf16[128,1024]{1,0:T(8,128)(2,1)}, f32[352,1024]{1,0:T(8,128)}, bf16[2,4,128,704]{3,2,1,0:T(8,128)(2,1)}) custom-call(bf16[16,128,1024]{2,1,0:T(8,128)(2,1)} %get-tuple-element.61.routed, f32[128,1024]{1,0:T(8,128)} %get-tuple-element.62.middle, f32[128,1]{1,0:T(8,128)} %reshape.237.keep, bf16[2,4,128,704]{3,2,1,0:T(8,128)(2,1)} %bitcast.81, ...), custom_call_target="tpu_custom_call" | custom-call | tf_op jit(solution)/shard_map/pallas_call | solution.py:589
  508.2 1.6 slice_convert_fusion
  509.9 1.6 copy.81
  516.6 1.7 copy.95
  (65 shorter events, 26.2 us)
Async XLA Ops:
  0.6 3.5 copy-start
  0.7 4.1 copy-start.3
  0.7 5.7 %copy-start.9 = (s32[2]{0:T(128)S(1)}, s32[2]{0:T(128)}, u32[]{:S(2)}) copy-start(s32[2]{0:T(128)} %param.19) | copy-start | bytes 28
  0.7 6.3 %copy-start.8 = (s32[2,64,2]{1,2,0:T(2,128)S(1)}, s32[2,64,2]{1,2,0:T(2,128)}, u32[]{:S(2)}) copy-start(s32[2,64,2]{1,2,0:T(2,128)} %param.20) | copy-start | bytes 3076
  62.8 11.0 %copy-start.5 = (f32[1024,4]{0,1:T(4,128)S(1)}, f32[1024,4]{0,1:T(4,128)}, u32[]{:S(2)}) copy-start(f32[1024,4]{0,1:T(4,128)} %param.29) | copy-start | bytes 49156
  225.4 18.5 %copy-start.6 = (f32[8,1024]{1,0:T(8,128)S(1)}, f32[8,1024]{1,0:T(8,128)}, u32[]{:S(2)}) copy-start(f32[8,1024]{1,0:T(8,128)} %get-tuple-element.78) | copy-start | bytes 98308
  369.2 2.6 copy-start.7
  515.0 3.2 copy-start.4
  515.0 4.0 copy-start.2
  516.6 3.6 copy-start.1
